TPU v7x, 512 devices: a whole 4x8x8 slice. The times are simulated.
512 devices in a mesh: section: 64 (over z_lo, x, y), tp: 8 (over z_hi, core).
Axes of the slice: x: 4, y: 8, z: 8 (z_hi: 4, z_lo: 2; z = z_hi * 2 + z_lo), core: 2. Of those that a mesh axis runs over, the one named last changes fastest.
Arguments:
- ctx_keys: bfloat16 [64, 6144, 1024], P('section', None, 'tp'), may hold values from -6 to 6
- ctx_values: bfloat16 [64, 6144, 1024], P('section', None, 'tp'), may hold values from -6 to 6
- span_q: bfloat16 [64, 64, 8192], P('section', None, 'tp'), may hold values from -140 to 140
- span_k: bfloat16 [64, 64, 1024], P('section', None, 'tp'), may hold values from -6 to 6
- span_v: bfloat16 [64, 64, 1024], P('section', None, 'tp'), may hold values from -6 to 6
- lengths: int32 [64], P('section'), may hold values from 768 to 6144, as said below
- group_lists: int32 [64, 4], replicated, may hold values from 0 to 63, as said below
- dec_q: bfloat16 [256, 2, 8192], P('section', None, 'tp'), may hold values from -140 to 140
- dec_k: bfloat16 [256, 2, 1024], P('section', None, 'tp'), may hold values from -6 to 6
- dec_v: bfloat16 [256, 2, 1024], P('section', None, 'tp'), may hold values from -6 to 6
- out_weight: bfloat16 [8192, 8192], P('tp', 'section'), may hold values from -0.0625 to 0.0625
Outputs:
- span_out: bfloat16 [64, 64, 8192], P('section', None, 'tp')
- dec_proj: bfloat16 [256, 2, 8192], P('tp', None, 'section')
Inputs may be any that keep to these rules, and one draw needn't show every extreme that they name: `group_lists`: each row names 4 distinct groups, and every group is named by exactly 4 prompts, each in a different column. `lengths`: some prompt has exactly 6144.
All inputs are finite; a program needn't handle non-finite values.
Results may differ from a plain program's by a relative error of at most 0.0057.
Values may be sent and summed in bfloat16 or wider, within the bound.
A program may use at most 64 MiB of HBM per device.

v0:
```python
import jax
import jax.numpy as jnp
from jax import lax
from jax.sharding import PartitionSpec as P

HD = 128


NEG = -1e30


def part_scores(query, keys):
    scale = float(query.shape[-1]) ** (-0.5)
    return jnp.einsum("rkgh,tkh->rkgt", query, keys, preferred_element_type=jnp.float32) * scale


def prompt_part(query, ctx_k, ctx_v, new_k, new_v, length, later):
    first = part_scores(query, ctx_k)
    second = part_scores(query, new_k)
    seen = (jnp.arange(ctx_k.shape[0]) < length)[None, None, None, :]
    top = jnp.maximum(
        jnp.max(jnp.where(seen, first, NEG), axis=-1),
        jnp.max(jnp.where(later, second, NEG), axis=-1),
    )
    weight_one = jnp.where(seen, jnp.exp(first - top[..., None]), 0.0)
    weight_two = jnp.where(later, jnp.exp(second - top[..., None]), 0.0)
    total = jnp.sum(weight_one, axis=-1) + jnp.sum(weight_two, axis=-1)
    numer = jnp.einsum(
        "rkgt,tkh->rkgh", weight_one.astype(jnp.bfloat16), ctx_v, preferred_element_type=jnp.float32
    )
    numer = numer + jnp.einsum(
        "rkgt,tkh->rkgh", weight_two.astype(jnp.bfloat16), new_v, preferred_element_type=jnp.float32
    )
    return (numer, top, total)


def body(
    ctx_keys,
    ctx_values,
    span_q,
    span_k,
    span_v,
    lengths,
    group_lists,
    dec_q,
    dec_k,
    dec_v,
    out_weight,
):
    heads_kv = ctx_keys.shape[-1] // HD
    group = span_q.shape[-1] // HD // heads_kv
    rows = span_q.shape[1]
    steps = dec_q.shape[1]
    cand = dec_q.shape[0]
    keys = ctx_keys[0].reshape(-1, heads_kv, HD)
    values = ctx_values[0].reshape(-1, heads_kv, HD)
    block_k = span_k[0].reshape(rows, heads_kv, HD)
    block_v = span_v[0].reshape(rows, heads_kv, HD)
    length = lengths[0]
    later = (jnp.arange(rows)[:, None] >= jnp.arange(rows)[None, :])[:, None, None, :]
    numer, top, total = prompt_part(
        span_q[0].reshape(rows, heads_kv, group, HD), keys, values, block_k, block_v, length, later
    )
    span_out = (numer / total[..., None]).reshape(1, rows, -1).astype(jnp.bfloat16)
    here = lax.axis_index("section")
    width = lax.axis_size("section")
    prompt_ids = jnp.arange(group_lists.shape[0], dtype=jnp.int32)
    senders = lax.dynamic_index_in_dim(group_lists, here, 0, keepdims=False)
    every_q, every_k, every_v = (
        lax.all_gather(dec_q, "section", axis=0, tiled=True),
        lax.all_gather(dec_k, "section", axis=0, tiled=True),
        lax.all_gather(dec_v, "section", axis=0, tiled=True),
    )
    wanted = senders * cand + jnp.arange(cand, dtype=jnp.int32)
    query_rows = jnp.take(every_q, wanted, axis=0)
    key_rows = jnp.take(every_k, wanted, axis=0)
    value_rows = jnp.take(every_v, wanted, axis=0)
    count = query_rows.shape[0]
    items = query_rows.shape[1]
    query = query_rows.reshape(count * items, heads_kv, group, HD)
    num_one, top_one, total_one = prompt_part(query, keys, values, block_k, block_v, length, True)
    num_one, top_one, total_one = (
        num_one.reshape(count, items, heads_kv, group, HD),
        top_one.reshape(count, items, heads_kv, group),
        total_one.reshape(count, items, heads_kv, group),
    )
    query = query_rows.reshape(cand, steps, heads_kv, group, HD)
    own_k = key_rows.reshape(cand, steps, heads_kv, HD)
    own_v = value_rows.reshape(cand, steps, heads_kv, HD)
    scale = float(HD) ** (-0.5)
    third = (
        jnp.einsum("cskgh,ctkh->cskgt", query, own_k, preferred_element_type=jnp.float32) * scale
    )
    causal = (jnp.arange(steps)[:, None] >= jnp.arange(steps)[None, :])[None, :, None, None, :]
    top_two = jnp.max(jnp.where(causal, third, NEG), axis=-1)
    weight = jnp.where(causal, jnp.exp(third - top_two[..., None]), 0.0)
    total_two = jnp.sum(weight, axis=-1)
    num_two = jnp.einsum(
        "cskgt,ctkh->cskgh", weight.astype(jnp.bfloat16), own_v, preferred_element_type=jnp.float32
    )
    top_all = jnp.maximum(top_one, top_two)
    factor_one = jnp.exp(top_one - top_all)
    factor_two = jnp.exp(top_two - top_all)
    mixed = (num_one * factor_one[..., None] + num_two * factor_two[..., None]) / (
        total_one * factor_one + total_two * factor_two
    )[..., None]
    dec_out = mixed.reshape(cand, steps, -1).astype(jnp.bfloat16)
    terms = jnp.einsum(
        "csh,hd->csd",
        lax.all_gather(dec_out, "section", axis=0, tiled=True),
        out_weight,
        preferred_element_type=jnp.float32,
    )
    cand_ids = jnp.arange(width * cand, dtype=jnp.int32)
    column = cand_ids % cand
    device = cand_ids // cand
    match = jnp.take(group_lists, column, axis=1) == device[None, :]
    owner = jnp.sum(jnp.where(match, prompt_ids[:, None], 0), axis=0)
    terms = jnp.take(terms, owner * cand + column, axis=0)
    dec_proj = lax.psum_scatter(terms, "tp", scatter_dimension=0, tiled=True).astype(jnp.bfloat16)
    return (span_out, dec_proj)


def solution(mesh):
    in_specs = (
        P("section", None, "tp"),
        P("section", None, "tp"),
        P("section", None, "tp"),
        P("section", None, "tp"),
        P("section", None, "tp"),
        P("section"),
        P(),
        P("section", None, "tp"),
        P("section", None, "tp"),
        P("section", None, "tp"),
        P("tp", "section"),
    )
    out_specs = (P("section", None, "tp"), P("tp", None, "section"))
    return jax.shard_map(body, mesh=mesh, in_specs=in_specs, out_specs=out_specs, check_vma=False)
```

profile of v0, /device:TPU:1, one launch (start us, length us, event | category | flops | bytes accessed | tf_op | source)
XLA Modules:
  0.0 675.8 jit_solution(10702361518335004864)
XLA Ops:
  7.2 0.0 copy-start
  7.2 0.0 all-gather.3.cloned.1.call-start
  7.2 0.7 all-gather.3.cloned.1.call-update
  7.9 0.0 all-gather.5.cloned.1.call-start
  8.6 0.9 copy.56
  9.6 0.9 multiply_reduce_fusion
  10.5 133.0 %all_gather.13 = bf16[256,2,128]{2,1,0:T(2,128)(2,1)S(1)} all-gather(bf16[4,2,128]{2,1,0:T(2,128)(2,1)} %param.21), channel_id=1, replica_groups=mesh['section'=64,'tp'=8] {'section'}, dimensions={0}, use_global_device_ids=true | all-gather | bytes 133120 | tf_op jit(solution)/shard_map/all_gather | solution.py:71
  143.4 0.6 gather_fusion.3
  144.0 1.0 select_reduce_fusion.1
  145.0 125.1 %all_gather.14 = bf16[256,2,128]{2,1,0:T(2,128)(2,1)S(1)} all-gather(bf16[4,2,128]{2,1,0:T(2,128)(2,1)} %param.22), channel_id=1, replica_groups=mesh['section'=64,'tp'=8] {'section'}, dimensions={0}, use_global_device_ids=true | all-gather | bytes 133120 | tf_op jit(solution)/shard_map/all_gather | solution.py:72
  270.1 0.6 gather_fusion.4
  270.6 0.0 copy-done
  270.6 0.0 copy-start.3
  270.7 2.2 fusion
  272.9 4.5 copy-done.2
  277.4 3.6 fusion.5
  281.0 1.8 gather_fusion.1
  282.8 0.1 broadcast_select_fusion.1
  282.9 0.0 copy-start.4
  282.9 0.7 select_reduce_fusion
  283.7 0.2 fusion.76
  283.9 1.9 fusion.8
  285.9 0.0 copy-start.5
  285.9 0.5 bitcast_reduce_fusion.1
  286.3 0.2 convolution_multiply_fusion.3
  286.6 0.1 fusion.54
  286.7 0.1 convert_bitcast_fusion
  286.8 0.2 fusion.43
  286.9 0.2 convolution_add_fusion.1
  287.1 0.2 fusion.21
  287.4 0.6 convert_element_type.50
  288.0 0.0 all-gather.5.cloned.1.call-update
  288.0 7.5 %bitcast_reduce_fusion = f32[64,8]{0,1:T(8,128)S(1)} fusion(f32[6144,64,8]{0,1,2:T(8,128)} %copy-done.2, f32[64,8]{0,1:T(8,128)S(1)} %max.57, pred[6144]{0:T(1024)(128)(4,1)S(1)} %iota_compare_fusion.1), kind=kLoop, calls=%fused_computation.5 | loop fusion | flops 12582400 | bytes 12593152 | tf_op jit(solution)/shard_map/reduce_sum | solution.py:27
  295.5 0.1 fusion.33
  295.6 0.0 copy-done.7
  295.6 0.2 fusion.24
  295.8 0.1 copy.44
  295.9 0.7 convert_element_type.45
  296.7 0.7 gather_fusion
  297.4 1.3 dynamic-slice
  299.5 0.2 select_reduce_fusion.2
  299.7 292.5 %all-gather.5.cloned.1.call-done = bf16[256,2,1024]{2,1,0:T(2,128)(2,1)} async-done(((bf16[4,2,1024]{2,1,0:T(2,128)(2,1)}), bf16[256,2,1024]{2,1,0:T(2,128)(2,1)}) %all-gather.5.cloned.1.call-update) | async-done | bytes 1048592 | tf_op jit(solution)/shard_map/all_gather | solution.py:110
  592.2 1.7 fusion.25
  593.9 0.2 copy.49
  594.1 1.0 gather_fusion.2
  595.1 0.3 broadcast_select_fusion
  595.4 72.8 %all-reduce.2 = bf16[256,2,128]{2,1,0:T(2,128)(2,1)S(1)} all-reduce(f32[256,2,128]{2,1,0:T(2,128)S(1)} %broadcast_select_fusion), channel_id=2, replica_groups=mesh['section'=64,'tp'=8] {'tp'}, use_global_device_ids=true, to_apply=%region_11.13.clone | all-reduce | flops 65536 | bytes 393216
  668.3 0.6 dynamic-slice_convert_fusion
  (32 shorter events, 0.2 us)
Async XLA Ops:
  7.2 263.5 %copy-start = (bf16[1,6144,128]{2,1,0:T(8,128)(2,1)S(1)}, bf16[1,6144,128]{2,1,0:T(8,128)(2,1)}, u32[]{:S(2)}) copy-start(bf16[1,6144,128]{2,1,0:T(8,128)(2,1)} %param.13) | copy-start | bytes 4718596
  7.2 273.8 %all-gather.3.cloned.1.call-start = ((), (), s32[]{:S(2)}) async-start(), calls=%async_computation | async-start | bytes 1064960 | tf_op jit(solution)/shard_map/all_gather | solution.py:70
  7.9 584.3 %all-gather.5.cloned.1.call-start = ((), (), s32[]{:S(2)}) async-start(), calls=%async_computation.1 | async-start | bytes 1064960 | tf_op jit(solution)/shard_map/all_gather | solution.py:110
  270.6 6.8 %copy-start.3 = (bf16[1,6144,128]{2,1,0:T(8,128)(2,1)S(1)}, bf16[1,6144,128]{2,1,0:T(8,128)(2,1)}, u32[]{:S(2)}) copy-start(bf16[1,6144,128]{2,1,0:T(8,128)(2,1)} %param.14) | copy-start | bytes 4718596
  272.9 4.6 copy-start.2
  282.9 0.8 copy-start.4
  285.9 1.1 copy-start.5
  288.0 7.6 %copy-start.7 = (f32[64,8,128]{2,0,1:T(8,128)S(1)}, f32[64,8,128]{2,0,1:T(8,128)}, u32[]{:S(2)}) copy-start(f32[64,8,128]{2,0,1:T(8,128)} %fusion.5) | copy-start | bytes 786436
  295.5 1.2 copy-start.1
  295.5 296.7 %copy-start.6 = (bf16[1024,128]{1,0:T(8,128)(2,1)S(1)}, bf16[1024,128]{1,0:T(8,128)(2,1)}, u32[]{:S(2)}) copy-start(bf16[1024,128]{1,0:T(8,128)(2,1)} %param.23) | copy-start | bytes 786436
Sparse Core Ops, SparseCore 0:
  10.1 260.0 all-gather.2
  288.1 304.0 all-gather.4
where the time goes:
time: 677 us; the launch traced here: 676 us
  blocking collectives  331 us (49%)
  waiting for transfers between devices  293 us (43%)
  between operations  15.7 us (2%)
  local copies, waits for them, and re-layouts  13.8 us (2%)
  matrix products  12.1 us (2%)
  other arithmetic  9.99 us (1%)
    all_gather x1, waiting for transfers between devices, body(): lax.all_gather(dec_out, 'section', axis=0, tiled=True)  292 us
    all_gather x1, blocking collectives, body(): lax.all_gather(dec_k, 'section', axis=0, tiled=True)  133 us
    all_gather x1, blocking collectives, body(): lax.all_gather(dec_v, 'section', axis=0, tiled=True)  125 us
    unnamed x1, blocking collectives  72.8 us
  transfers between devices with their start and end apart: 2, of which 1 were waited for; matrix products, arithmetic and copies ran while one was open for 3% of the time, Pallas kernels for 0%

commit v1 on v0

v1 whole, which is shorter than its diff:
```python
import math

import jax
import jax.numpy as jnp
from jax import lax
from jax.experimental import pallas as pl
from jax.experimental.pallas import tpu as pltpu
from jax.sharding import PartitionSpec as P

HD = 128
NX, NY, NZL, NZH = 4, 8, 2, 4
HEADS = 8
SPAN = 64
CHUNK = 1024
LOG2 = HD**-0.5 * math.log2(math.e)
NEG = -1e30
MESH = pl.DeviceIdType.MESH
NT = (((1,), (1,)), ((), ()))
TN = (((0,), (0,)), ((), ()))
NN = (((1,), (0,)), ((), ()))
NEAR = (0, 1, 7, 2, 6, 3, 5, 4)
NEAR_X = (1, 3, 2)


def dot(a, b, dims=NN):
    return lax.dot_general(a, b, dims, preferred_element_type=jnp.float32)


def iota(shape, dim):
    return lax.broadcasted_iota(jnp.int32, shape, dim)


def kernel(
    ck, cv, sq, sk, sv, length_ref, groups, dq, dk, dv, w_hbm,
    span_ref, proj_ref,
    k, v, svx, qs, m_s, acc_s, qf, kvf, g1, s2, r2, sel, msg, buf, w, pt, zs, rr,
    ksem, vsem, wsem, g1s, g1r, g2s, g2r, wss, wsr, p1s, p1r, p2s, p2r, cs, cr, rs, rrs,
):
    section, tp = lax.axis_index("section"), lax.axis_index("tp")
    zl, x, y = section // 32, lax.rem(section // NY, NX), lax.rem(section, NY)
    zh, core = tp // 2, lax.rem(tp, 2)
    block = section // NY

    def dev(sec, t):
        return {"section": sec, "tp": t}

    def remote(src, dst, ssem, rsem, device):
        return pltpu.make_async_remote_copy(
            src_ref=src, dst_ref=dst, send_sem=ssem, recv_sem=rsem, device_id=device, device_id_type=MESH
        )

    def yo(o):
        return lax.rem(y + o + NY, NY)

    def xo(o):
        return lax.rem(x + o + NX, NX)

    same = zl == core
    plane = core * 32 + x * NY
    turned = zh * 2 + zl

    barrier = pltpu.get_barrier_semaphore()

    def greet(device):
        pl.semaphore_signal(barrier, inc=1, device_id=device, device_id_type=MESH)

    for o in range(1, NY):
        greet(dev(block * NY + yo(o), tp))
    for o in range(1, NZL * NX):
        greet(dev(lax.rem(block + o, NZL * NX) * NY + y, tp))
    greet(dev(section, zh * 2 + 1 - core))

    @pl.when(jnp.logical_not(same))
    def _():
        for o in range(NY):
            greet(dev(plane + yo(o), turned))

    for zz in range(NZL):
        for hh in range(NZH):
            @pl.when(jnp.logical_not(jnp.logical_and(same, jnp.logical_and(zl == zz, zh == hh))))
            def _(zz=zz, hh=hh):
                greet(dev(zz * 32 + x * NY + y, hh * 2 + zl))

    nch = ck.shape[1] // CHUNK
    copies = []
    for i in range(nch):
        rows = pl.ds(i * CHUNK, CHUNK)
        a = pltpu.make_async_copy(ck.at[0, rows], k.at[rows], ksem.at[i])
        b = pltpu.make_async_copy(cv.at[0, rows], v.at[rows, pl.ds(0, HD)], vsem.at[i])
        a.start()
        b.start()
        copies.append((a, b))

    for j in range(4):
        piece = dq[j].astype(jnp.float32)
        for h in range(HEADS):
            qf[pl.ds(j * 16 + h, 2, stride=8), :] = piece[:, h * HD:(h + 1) * HD]
        kvf[2 * j:2 * j + 2, :] = dk[j].astype(jnp.float32)
        kvf[8 + 2 * j:10 + 2 * j, :] = dv[j].astype(jnp.float32)
    g1[y, 0:64, :] = qf[...].astype(jnp.bfloat16)
    g1[y, 64:80, :] = kvf[...].astype(jnp.bfloat16)

    for h in range(HEADS):
        qs[h * SPAN:(h + 1) * SPAN, :] = sq[0, :, h * HD:(h + 1) * HD]
    svx[:, 0:HD] = sv[0]
    svx[:, HD:] = jnp.ones((SPAN, HD), jnp.bfloat16)
    n_rows = HEADS * SPAN
    first = dot(qs[...], sk[0], NT)
    shape = (n_rows, SPAN)
    first = jnp.where(iota(shape, 1) <= (iota(shape, 0) & (SPAN - 1)), first, NEG)
    top = jnp.max(first, axis=1, keepdims=True) * LOG2
    weights = jnp.exp2(first * LOG2 - top)
    acc_s[...] = dot(weights.astype(jnp.bfloat16), svx[...])
    m_s[...] = jnp.broadcast_to(top, m_s.shape)
    length = length_ref[0]

    def span_chunk(i):
        copies[i][0].wait()
        copies[i][1].wait()
        rows = pl.ds(i * CHUNK, CHUNK)
        seen = jnp.where(iota((CHUNK, HD), 0) + i * CHUNK < length, 1.0, 0.0).astype(jnp.bfloat16)
        kc = k[rows, :] * seen + k[0:1, :] * (1 - seen)
        k[rows, :] = kc
        v[rows, 0:HD] = v[rows, 0:HD] * seen
        v[rows, HD:] = seen
        s = dot(qs[...], kc, NT)
        old = m_s[...]
        new = jnp.maximum(old, jnp.max(s, axis=1, keepdims=True) * LOG2)
        p = jnp.exp2(s * LOG2 - new[:, 0:1])
        shrink = jnp.exp2(old - new)
        m_s[...] = new
        part = dot(p.astype(jnp.bfloat16), v[rows, :])
        acc_s[:, 0:HD] = acc_s[:, 0:HD] * shrink + part[:, 0:HD]
        acc_s[:, HD:] = acc_s[:, HD:] * shrink + part[:, HD:]

    for i in range(0, 2):
        span_chunk(i)

    pl.semaphore_wait(
        barrier, (NY - 1) + (NZL * NX - 1) + 1 + jnp.where(same, NZL * NZH - 1, NY + NZL * NZH)
    )

    sent = []
    for o in NEAR[1:]:
        c = remote(g1.at[y], g1.at[y], g1s.at[o], g1r.at[o], dev(block * NY + yo(o), tp))
        c.start()
        sent.append(c)
    w_copy = pltpu.make_async_copy(w_hbm, w, wsem)
    w_swap = remote(w_hbm, w, wss, wsr, dev(plane + y, turned))

    @pl.when(same)
    def _():
        w_copy.start()

    @pl.when(jnp.logical_not(same))
    def _():
        w_swap.start()

    for i in range(2, nch):
        span_chunk(i)

    for h in range(HEADS):
        rows = slice(h * SPAN, (h + 1) * SPAN)
        span_ref[0, :, h * HD:(h + 1) * HD] = (acc_s[rows, 0:HD] / acc_s[rows, HD:]).astype(jnp.bfloat16)

    for o in NEAR[1:]:
        slot = yo(-o)
        remote(g1.at[slot], g1.at[slot], g1s.at[o], g1r.at[o], dev(block * NY + yo(o), tp)).wait_recv()

    owner_of = (iota((16, HD), 0) & 7) // 2
    sent2 = []
    for o in (1, 7, 2, 6, 3, 5, 4, 0):
        to = lax.rem(block + o, NZL * NX)
        own = jnp.zeros((16, HD), jnp.float32)
        for j in range(4):
            at = groups[to * NY + y, j] & (NY - 1)
            s2[to, j * 16:(j + 1) * 16, :] = g1[at, j * 16:(j + 1) * 16, :]
            own = jnp.where(owner_of == j, g1[at, 64:80, :].astype(jnp.float32), own)
        s2[to, 64:80, :] = own.astype(jnp.bfloat16)
        if o:
            c = remote(s2.at[to], r2.at[block], g2s.at[o], g2r.at[o], dev(to * NY + y, tp))
            c.start()
            sent2.append(c)
    r2[block] = s2[block]

    lane = iota((16, 512), 1)
    sub = iota((16, 512), 0)
    col = (sub & 7) // 2

    def one_hot(i, _):
        want = jnp.zeros((16, 512), jnp.int32)
        for half in range(2):
            for j in range(4):
                want = jnp.where(
                    jnp.logical_and(sub // 8 == half, col == j), groups[2 * i + half, j], want
                )
        hit = want * 8 + (sub & 7) == lane
        pt[pl.ds(pl.multiple_of(i * 16, 16), 16), :] = jnp.where(hit, 1.0, 0.0).astype(jnp.bfloat16)
        return 0

    lax.fori_loop(0, 32, one_hot, 0)

    for o in range(1, NZL * NX):
        slot = lax.rem(block + NZL * NX - o, NZL * NX)
        remote(s2.at[slot], r2.at[slot], g2s.at[o], g2r.at[o], dev(slot * NY + y, tp)).wait_recv()
    own = jnp.zeros((16, HD), jnp.float32)
    for j in range(4):
        at = lax.shift_right_logical(groups[section, j], 3)
        qf[j * 16:(j + 1) * 16, :] = r2[at, j * 16:(j + 1) * 16, :].astype(jnp.float32)
        own = jnp.where(owner_of == j, r2[at, 64:80, :].astype(jnp.float32), own)

    for h in range(0, HEADS, 2):
        pair = [qf[pl.ds(h + e, 8, stride=8), :] for e in range(2)]
        sel[h * 8:h * 8 + 16, :] = jnp.concatenate(pair, axis=0).astype(jnp.bfloat16)
    query = sel[...]
    own_k = own.astype(jnp.bfloat16)
    own_v = jnp.concatenate([own[8:16], own[0:8]], axis=0).astype(jnp.bfloat16)
    own_v = jnp.concatenate([own_v, jnp.ones((16, HD), jnp.bfloat16)], axis=1)
    s_ctx = dot(query, k[...], NT)
    s_blk = dot(query, sk[0], NT)
    s_own = dot(query, own_k, NT)
    r16, c16 = iota((64, 16), 0), iota((64, 16), 1)
    fits = jnp.logical_and(c16 // 2 == (r16 // 2) % 4, c16 % 2 <= r16 % 2)
    s_own = jnp.where(fits, s_own, NEG)
    top = jnp.maximum(
        jnp.maximum(jnp.max(s_ctx, axis=1, keepdims=True), jnp.max(s_blk, axis=1, keepdims=True)),
        jnp.max(s_own, axis=1, keepdims=True),
    ) * LOG2
    total = dot(jnp.exp2(s_ctx * LOG2 - top).astype(jnp.bfloat16), v[...])
    total += dot(jnp.exp2(s_blk * LOG2 - top).astype(jnp.bfloat16), svx[...])
    total += dot(jnp.exp2(s_own * LOG2 - top).astype(jnp.bfloat16), own_v)
    msg[...] = (total[:, 0:HD] / total[:, HD:]).astype(jnp.bfloat16)

    sent3 = []
    for o in NEAR:
        c = remote(msg, buf.at[section], p1s.at[o], p1r.at[o], dev(plane + yo(o), turned))
        if o:
            c.start()
            sent3.append(c)
        else:
            pl.when(jnp.logical_not(same))(c.start)

            @pl.when(same)
            def _():
                buf[section] = msg[...]

    def sibling(slot, i):
        return remote(buf.at[slot], buf.at[slot], cs.at[i], cr.at[i], dev(section, zh * 2 + 1 - core))

    for o in NEAR:
        slot = plane + yo(-o)
        c = remote(msg, buf.at[slot], p1s.at[o], p1r.at[o], dev(plane + yo(o), turned))
        if o:
            c.wait_recv()
        else:
            pl.when(jnp.logical_not(same))(c.wait_recv)
        for d in NEAR_X:
            c = remote(
                buf.at[slot], buf.at[slot], p2s.at[o, d], p2r.at[o, d],
                dev(zl * 32 + xo(d) * NY + y, tp),
            )
            c.start()
            sent3.append(c)
        c = sibling(slot, o * 4)
        c.start()
        sent3.append(c)
    for o in NEAR:
        for d in NEAR_X:
            slot = core * 32 + xo(-d) * NY + yo(-o)
            remote(
                buf.at[slot], buf.at[slot], p2s.at[o, d], p2r.at[o, d],
                dev(zl * 32 + xo(d) * NY + y, tp),
            ).wait_recv()
            c = sibling(slot, o * 4 + d)
            c.start()
            sent3.append(c)
    for o in NEAR:
        for d in (0, *NEAR_X):
            slot = (1 - core) * 32 + xo(-d) * NY + yo(-o)
            sibling(slot, o * 4 + d).wait_recv()

    pl.when(same)(w_copy.wait)
    pl.when(jnp.logical_not(same))(w_swap.wait_recv)
    full = None
    for pair in range(HEADS // 2):
        at = pair * 2 * HD
        both = jnp.concatenate([w[at:at + HD, :], w[at + HD:at + 2 * HD, :]], axis=1)
        part = dot(buf[:, pair * 16:(pair + 1) * 16, :].reshape(1024, HD), both)
        full = part if full is None else full + part
    full = full.reshape(64, 16, 2 * HD)
    rows = (full[:, 0:8, 0:HD] + full[:, 8:16, HD:]).reshape(512, HD).astype(jnp.bfloat16)
    zs[...] = dot(pt[...], rows, TN).astype(jnp.bfloat16)

    sent4 = []
    for t in range(8):
        c = remote(
            zs.at[pl.ds(t * 64, 64)], rr.at[turned], rs.at[t], rrs.at[turned], dev(plane + y, t)
        )
        mine = jnp.logical_and(same, tp == t)
        pl.when(jnp.logical_not(mine))(c.start)

        @pl.when(mine)
        def _(t=t):
            rr[turned] = zs[t * 64:(t + 1) * 64, :]

        sent4.append((c, mine))
    out = None
    for s in range(8):
        c = remote(zs.at[pl.ds(s * 64, 64)], rr.at[s], rs.at[s], rrs.at[s], dev(plane + y, s))
        pl.when(jnp.logical_not(jnp.logical_and(same, turned == s)))(c.wait_recv)
    for s in range(8):
        part = rr[s].astype(jnp.float32)
        out = part if out is None else out + part
    proj_ref[...] = out.astype(jnp.bfloat16)

    for c in sent + sent2 + sent3:
        c.wait_send()
    pl.when(jnp.logical_not(same))(w_swap.wait_send)
    c = remote(msg, buf.at[section], p1s.at[0], p1r.at[0], dev(plane + y, turned))
    pl.when(jnp.logical_not(same))(c.wait_send)
    for c, mine in sent4:
        pl.when(jnp.logical_not(mine))(c.wait_send)


def body(ctx_keys, ctx_values, span_q, span_k, span_v, lengths, group_lists, dec_q, dec_k, dec_v, out_weight):
    ctx = ctx_keys.shape[1]
    bf, f32 = jnp.bfloat16, jnp.float32
    vmem = pl.BlockSpec(memory_space=pltpu.VMEM)
    smem = pl.BlockSpec(memory_space=pltpu.SMEM)
    hbm = pl.BlockSpec(memory_space=pltpu.HBM)
    dma = pltpu.SemaphoreType.DMA
    span_out, proj = pl.pallas_call(
        kernel,
        name="block_and_decode_attention",
        out_shape=(
            jax.ShapeDtypeStruct(span_q.shape, bf),
            jax.ShapeDtypeStruct((64, HD), bf),
        ),
        in_specs=[hbm, hbm, vmem, vmem, vmem, smem, smem, vmem, vmem, vmem, hbm],
        out_specs=(vmem, vmem),
        scratch_shapes=[
            pltpu.VMEM((ctx, HD), bf),
            pltpu.VMEM((ctx, 2 * HD), bf),
            pltpu.VMEM((SPAN, 2 * HD), bf),
            pltpu.VMEM((HEADS * SPAN, HD), bf),
            pltpu.VMEM((HEADS * SPAN, HD), f32),
            pltpu.VMEM((HEADS * SPAN, 2 * HD), f32),
            pltpu.VMEM((64, HD), f32),
            pltpu.VMEM((16, HD), f32),
            pltpu.VMEM((8, 80, HD), bf),
            pltpu.VMEM((8, 80, HD), bf),
            pltpu.VMEM((8, 80, HD), bf),
            pltpu.VMEM((64, HD), bf),
            pltpu.VMEM((64, HD), bf),
            pltpu.VMEM((64, 64, HD), bf),
            pltpu.VMEM((HEADS * HD, HD), bf),
            pltpu.VMEM((512, 512), bf),
            pltpu.VMEM((512, HD), bf),
            pltpu.VMEM((8, 64, HD), bf),
            dma((ctx // CHUNK,)), dma((ctx // CHUNK,)), dma,
            dma((8,)), dma((8,)), dma((8,)), dma((8,)), dma, dma,
            dma((8,)), dma((8,)), dma((8, 4)), dma((8, 4)), dma((32,)), dma((32,)),
            dma((8,)), dma((8,)),
        ],
        compiler_params=pltpu.CompilerParams(
            collective_id=0, has_side_effects=True, vmem_limit_bytes=48 << 20
        ),
        cost_estimate=pl.CostEstimate(flops=2_000_000_000, bytes_accessed=4 << 20, transcendentals=3_600_000),
    )(
        ctx_keys, ctx_values, span_q, span_k, span_v, lengths, group_lists, dec_q, dec_k, dec_v, out_weight
    )
    return span_out, proj.reshape(32, 2, HD)


def solution(mesh):
    in_specs = (
        P("section", None, "tp"),
        P("section", None, "tp"),
        P("section", None, "tp"),
        P("section", None, "tp"),
        P("section", None, "tp"),
        P("section"),
        P(),
        P("section", None, "tp"),
        P("section", None, "tp"),
        P("section", None, "tp"),
        P("tp", "section"),
    )
    out_specs = (P("section", None, "tp"), P("tp", None, "section"))
    return jax.shard_map(body, mesh=mesh, in_specs=in_specs, out_specs=out_specs, check_vma=False)
```

time: 677 us -> 63.3 us (0.09)
  blocking collectives: 331 us -> 0 us
  waiting for transfers between devices: 293 us -> 0 us
  Pallas kernels: 0 us -> 51.3 us
  between operations: 15.7 us -> 1.29 us
  matrix products: 12.1 us -> 0 us
  other arithmetic: 9.99 us -> 0 us
    all_gather x2 -> x0, waiting for transfers between devices: 292 us -> none  [the longest x1 292 us: body(): lax.all_gather(dec_out, 'section', axis=0, tiled=True)]
    all_gather x2 -> x0, blocking collectives: 258 us -> none  [the longest x1 133 us: body(): lax.all_gather(dec_k, 'section', axis=0, tiled=True)]
    unnamed x1 -> x0, blocking collectives: 72.8 us -> none
    pallas_call x0 -> x1, Pallas kernels: none -> 51.3 us  [body(): pl.pallas_call(kernel, name='block_and_decode_attention', out_shape=(jax....]
    dot_general x11 -> x0, matrix products: 12.1 us -> none  [the longest x2 5.47 us: prompt_part(): jnp.einsum('rkgt,tkh->rkgh', weight_one.astype(jnp.bfloat16), ctx_v, pref...]
    reduce_sum x5 -> x0, other arithmetic: 8.38 us -> none  [the longest x4 8.17 us: prompt_part(): total = jnp.sum(weight_one, axis=-1) + jnp.sum(weight_two, axis=-1)]
  transfers between devices with their start and end apart: 2 -> 0, of which waited for: 1 -> 0; matrix products, arithmetic and copies ran while one was open for 3% -> 0% of each run, Pallas kernels for 0% -> 0%
where the time goes in v1:
time: 63.3 us; the launch traced here: 62.8 us
  Pallas kernels  51.3 us (81%)
  local copies, waits for them, and re-layouts  10.2 us (16%)
  between operations  1.29 us (2%)
    pallas_call x1, Pallas kernels, body(): pl.pallas_call(kernel, name='block_and_decode_attention', out_shape=(jax....  51.3 us
    unnamed x21, local copies, waits for them, and re-layouts  10.2 us

profile of v1, /device:TPU:1, one launch (start us, length us, event | category | flops | bytes accessed | tf_op | source)
XLA Modules:
  0.0 62.8 jit_solution(7413681626924609389)
XLA Ops:
  1.3 0.8 %copy.13.groups = s32[64,4]{1,0:T(8,128)S(1)} copy(s32[64,4]{0,1:T(4,128)} %param.17) | data formatting | bytes 2048 | tf_op args[6]
  2.0 0.0 copy-start
  2.0 1.4 %copy-done = bf16[1,6144,128]{2,1,0:T(8,128)(2,1)S(1)} copy-done((bf16[1,6144,128]{2,1,0:T(8,128)(2,1)S(1)}, bf16[1,6144,128]{2,1,0:T(8,128)(2,1)}, u32[]{:S(2)}) %copy-start) | copy-done | bytes 1572888
  3.5 0.0 copy-start.1
  3.5 1.4 %copy-done.1 = bf16[1,6144,128]{2,1,0:T(8,128)(2,1)S(1)} copy-done((bf16[1,6144,128]{2,1,0:T(8,128)(2,1)S(1)}, bf16[1,6144,128]{2,1,0:T(8,128)(2,1)}, u32[]{:S(2)}) %copy-start.1) | copy-done | bytes 1572888
  4.9 0.0 copy-start.2
  4.9 0.9 %copy-done.2 = bf16[1024,128]{1,0:T(8,128)(2,1)S(1)} copy-done((bf16[1024,128]{1,0:T(8,128)(2,1)S(1)}, bf16[1024,128]{1,0:T(8,128)(2,1)}, u32[]{:S(2)}) %copy-start.2) | copy-done | bytes 262168
  5.8 0.0 copy-start.3
  5.8 0.9 %copy-done.3 = bf16[1,64,1024]{2,1,0:T(8,128)(2,1)S(1)} copy-done((bf16[1,64,1024]{2,1,0:T(8,128)(2,1)S(1)}, bf16[1,64,1024]{2,1,0:T(8,128)(2,1)}, u32[]{:S(2)}) %copy-start.3) | copy-done | bytes 131096
  6.7 0.0 copy-start.4
  6.7 0.7 %copy-done.4 = bf16[1,64,128]{2,1,0:T(8,128)(2,1)S(1)} copy-done((bf16[1,64,128]{2,1,0:T(8,128)(2,1)S(1)}, bf16[1,64,128]{2,1,0:T(8,128)(2,1)}, u32[]{:S(2)}) %copy-start.4) | copy-done | bytes 16408
  7.4 0.0 copy-start.5
  7.4 0.7 %copy-done.5 = bf16[1,64,128]{2,1,0:T(8,128)(2,1)S(1)} copy-done((bf16[1,64,128]{2,1,0:T(8,128)(2,1)S(1)}, bf16[1,64,128]{2,1,0:T(8,128)(2,1)}, u32[]{:S(2)}) %copy-start.5) | copy-done | bytes 16408
  8.2 0.0 copy-start.6
  8.2 0.7 %copy-done.6 = bf16[4,2,1024]{2,1,0:T(2,128)(2,1)S(1)} copy-done((bf16[4,2,1024]{2,1,0:T(2,128)(2,1)S(1)}, bf16[4,2,1024]{2,1,0:T(2,128)(2,1)}, u32[]{:S(2)}) %copy-start.6) | copy-done | bytes 16408
  8.9 0.0 copy-start.7
  8.9 0.7 %copy-done.7 = bf16[4,2,128]{2,1,0:T(2,128)(2,1)S(1)} copy-done((bf16[4,2,128]{2,1,0:T(2,128)(2,1)S(1)}, bf16[4,2,128]{2,1,0:T(2,128)(2,1)}, u32[]{:S(2)}) %copy-start.7) | copy-done | bytes 2072
  9.6 0.0 copy-start.8
  9.6 0.7 %copy-done.8 = bf16[4,2,128]{2,1,0:T(2,128)(2,1)S(1)} copy-done((bf16[4,2,128]{2,1,0:T(2,128)(2,1)S(1)}, bf16[4,2,128]{2,1,0:T(2,128)(2,1)}, u32[]{:S(2)}) %copy-start.8) | copy-done | bytes 2072
  10.2 51.3 %block_and_decode_attention.1 = (bf16[1,64,1024]{2,1,0:T(8,128)(2,1)S(1)}, bf16[64,128]{1,0:T(8,128)(2,1)S(1)}) custom-call(bf16[1,6144,128]{2,1,0:T(8,128)(2,1)S(1)} %copy-done, bf16[1,6144,128]{2,1,0:T(8,128)(2,1)S(1)} %copy-done.1, bf16[1,64,1024]{2,1,0:T(8,128)(2,1)S(1)} %copy-done.3, bf16[1,64,128]{2,1,0:T(8,128)(2,1)S(1)} %copy-done.4, ...), custom_call_target="tpu_custom_call" | custom-call | flops 2000000000 | bytes 4194304 | tf_op jit(solution)/shard_map/block_and_decode_attention/pallas_call | solution.py:332
  61.5 0.7 %copy.17 = bf16[1,64,1024]{2,1,0:T(8,128)(2,1)} copy(bf16[1,64,1024]{2,1,0:T(8,128)(2,1)S(1)} %get-tuple-element.8) | data formatting | bytes 262144
  62.2 0.6 copy.18
Async XLA Ops:
  2.0 1.4 %copy-start = (bf16[1,6144,128]{2,1,0:T(8,128)(2,1)S(1)}, bf16[1,6144,128]{2,1,0:T(8,128)(2,1)}, u32[]{:S(2)}) copy-start(bf16[1,6144,128]{2,1,0:T(8,128)(2,1)} %ck.1) | copy-start | bytes 4718596
  3.5 1.4 %copy-start.1 = (bf16[1,6144,128]{2,1,0:T(8,128)(2,1)S(1)}, bf16[1,6144,128]{2,1,0:T(8,128)(2,1)}, u32[]{:S(2)}) copy-start(bf16[1,6144,128]{2,1,0:T(8,128)(2,1)} %cv.1) | copy-start | bytes 4718596
  4.9 0.9 %copy-start.2 = (bf16[1024,128]{1,0:T(8,128)(2,1)S(1)}, bf16[1024,128]{1,0:T(8,128)(2,1)}, u32[]{:S(2)}) copy-start(bf16[1024,128]{1,0:T(8,128)(2,1)} %w_hbm.1) | copy-start | bytes 786436
  5.8 0.9 %copy-start.3 = (bf16[1,64,1024]{2,1,0:T(8,128)(2,1)S(1)}, bf16[1,64,1024]{2,1,0:T(8,128)(2,1)}, u32[]{:S(2)}) copy-start(bf16[1,64,1024]{2,1,0:T(8,128)(2,1)} %sq.1) | copy-start | bytes 393220
  6.7 0.7 %copy-start.4 = (bf16[1,64,128]{2,1,0:T(8,128)(2,1)S(1)}, bf16[1,64,128]{2,1,0:T(8,128)(2,1)}, u32[]{:S(2)}) copy-start(bf16[1,64,128]{2,1,0:T(8,128)(2,1)} %sk.1) | copy-start | bytes 49156
  7.4 0.7 %copy-start.5 = (bf16[1,64,128]{2,1,0:T(8,128)(2,1)S(1)}, bf16[1,64,128]{2,1,0:T(8,128)(2,1)}, u32[]{:S(2)}) copy-start(bf16[1,64,128]{2,1,0:T(8,128)(2,1)} %sv.1) | copy-start | bytes 49156
  8.2 0.7 %copy-start.6 = (bf16[4,2,1024]{2,1,0:T(2,128)(2,1)S(1)}, bf16[4,2,1024]{2,1,0:T(2,128)(2,1)}, u32[]{:S(2)}) copy-start(bf16[4,2,1024]{2,1,0:T(2,128)(2,1)} %dq.1) | copy-start | bytes 49156
  8.9 0.7 %copy-start.7 = (bf16[4,2,128]{2,1,0:T(2,128)(2,1)S(1)}, bf16[4,2,128]{2,1,0:T(2,128)(2,1)}, u32[]{:S(2)}) copy-start(bf16[4,2,128]{2,1,0:T(2,128)(2,1)} %dk.1) | copy-start | bytes 6148
  9.6 0.7 %copy-start.8 = (bf16[4,2,128]{2,1,0:T(2,128)(2,1)S(1)}, bf16[4,2,128]{2,1,0:T(2,128)(2,1)}, u32[]{:S(2)}) copy-start(bf16[4,2,128]{2,1,0:T(2,128)(2,1)} %dv.1) | copy-start | bytes 6148

commit v2 on v1

--- a/solution.py
+++ b/solution.py
@@ -1,3 +1,4 @@
+import functools
 import math
 
 import jax
@@ -20,6 +21,7 @@
 NN = (((1,), (0,)), ((), ()))
 NEAR = (0, 1, 7, 2, 6, 3, 5, 4)
 NEAR_X = (1, 3, 2)
+FAR = (4, 3, 5, 2, 6, 1, 7)
 
 
 def dot(a, b, dims=NN):
@@ -31,9 +33,10 @@
 
 
 def kernel(
-    ck, cv, sq, sk, sv, length_ref, groups, dq, dk, dv, w_hbm,
+    length_ref, ck, cv, sq_hbm, sk_hbm, sv_hbm, groups_hbm, dq_hbm, dk_hbm, dv_hbm, w_hbm,
     span_ref, proj_ref,
-    k, v, svx, qs, m_s, acc_s, qf, kvf, g1, s2, r2, sel, msg, buf, w, pt, zs, rr,
+    sq, sk, svx, groups, dq, dk, dv, insem,
+    k, v, qs, m_s, acc_s, qf, kvf, g1, s2, r2, sel, msg, buf, w, pt, zp, zs, rr,
     ksem, vsem, wsem, g1s, g1r, g2s, g2r, wss, wsr, p1s, p1r, p2s, p2r, cs, cr, rs, rrs,
 ):
     section, tp = lax.axis_index("section"), lax.axis_index("tp")
@@ -56,8 +59,18 @@
         return lax.rem(x + o + NX, NX)
 
     same = zl == core
+    buf4 = buf.reshape(NZL, NX, NY, 64, HD)
     plane = core * 32 + x * NY
     turned = zh * 2 + zl
+
+    small = []
+    for i, (src, dst) in enumerate((
+        (dq_hbm, dq), (dk_hbm, dk), (dv_hbm, dv), (sq_hbm.at[0], sq), (sk_hbm.at[0], sk),
+        (sv_hbm.at[0], svx.at[:, pl.ds(0, HD)]), (groups_hbm, groups),
+    )):
+        c = pltpu.make_async_copy(src, dst, insem.at[i])
+        c.start()
+        small.append(c)
 
     barrier = pltpu.get_barrier_semaphore()
 
@@ -82,15 +95,20 @@
                 greet(dev(zz * 32 + x * NY + y, hh * 2 + zl))
 
     nch = ck.shape[1] // CHUNK
-    copies = []
+
+    def chunk_copies(i):
+        rows = pl.ds(i * CHUNK, CHUNK)
+        return (
+            pltpu.make_async_copy(ck.at[0, rows], k.at[rows], ksem.at[i]),
+            pltpu.make_async_copy(cv.at[0, rows], v.at[rows, pl.ds(0, HD)], vsem.at[i]),
+        )
+
     for i in range(nch):
-        rows = pl.ds(i * CHUNK, CHUNK)
-        a = pltpu.make_async_copy(ck.at[0, rows], k.at[rows], ksem.at[i])
-        b = pltpu.make_async_copy(cv.at[0, rows], v.at[rows, pl.ds(0, HD)], vsem.at[i])
-        a.start()
-        b.start()
-        copies.append((a, b))
-
+        for c in chunk_copies(i):
+            c.start()
+
+    for c in small[:3]:
+        c.wait()
     for j in range(4):
         piece = dq[j].astype(jnp.float32)
         for h in range(HEADS):
@@ -100,12 +118,33 @@
     g1[y, 0:64, :] = qf[...].astype(jnp.bfloat16)
     g1[y, 64:80, :] = kvf[...].astype(jnp.bfloat16)
 
+    pl.semaphore_wait(
+        barrier, (NY - 1) + (NZL * NX - 1) + 1 + jnp.where(same, NZL * NZH - 1, NY + NZL * NZH)
+    )
+
+    sent = []
+    for o in FAR:
+        c = remote(g1.at[y], g1.at[y], g1s.at[o], g1r.at[o], dev(block * NY + yo(o), tp))
+        c.start()
+        sent.append(c)
+    w_copy = pltpu.make_async_copy(w_hbm, w, wsem)
+    w_swap = remote(w_hbm, w, wss, wsr, dev(plane + y, turned))
+
+    @pl.when(same)
+    def _():
+        w_copy.start()
+
+    @pl.when(jnp.logical_not(same))
+    def _():
+        w_swap.start()
+
+    for c in small[3:]:
+        c.wait()
     for h in range(HEADS):
-        qs[h * SPAN:(h + 1) * SPAN, :] = sq[0, :, h * HD:(h + 1) * HD]
-    svx[:, 0:HD] = sv[0]
+        qs[h * SPAN:(h + 1) * SPAN, :] = sq[:, h * HD:(h + 1) * HD]
     svx[:, HD:] = jnp.ones((SPAN, HD), jnp.bfloat16)
     n_rows = HEADS * SPAN
-    first = dot(qs[...], sk[0], NT)
+    first = dot(qs[...], sk[...], NT)
     shape = (n_rows, SPAN)
     first = jnp.where(iota(shape, 1) <= (iota(shape, 0) & (SPAN - 1)), first, NEG)
     top = jnp.max(first, axis=1, keepdims=True) * LOG2
@@ -115,9 +154,9 @@
     length = length_ref[0]
 
     def span_chunk(i):
-        copies[i][0].wait()
-        copies[i][1].wait()
         rows = pl.ds(i * CHUNK, CHUNK)
+        for c in chunk_copies(i):
+            c.wait()
         seen = jnp.where(iota((CHUNK, HD), 0) + i * CHUNK < length, 1.0, 0.0).astype(jnp.bfloat16)
         kc = k[rows, :] * seen + k[0:1, :] * (1 - seen)
         k[rows, :] = kc
@@ -133,35 +172,8 @@
         acc_s[:, 0:HD] = acc_s[:, 0:HD] * shrink + part[:, 0:HD]
         acc_s[:, HD:] = acc_s[:, HD:] * shrink + part[:, HD:]
 
-    for i in range(0, 2):
+    for i in range(nch - 1):
         span_chunk(i)
-
-    pl.semaphore_wait(
-        barrier, (NY - 1) + (NZL * NX - 1) + 1 + jnp.where(same, NZL * NZH - 1, NY + NZL * NZH)
-    )
-
-    sent = []
-    for o in NEAR[1:]:
-        c = remote(g1.at[y], g1.at[y], g1s.at[o], g1r.at[o], dev(block * NY + yo(o), tp))
-        c.start()
-        sent.append(c)
-    w_copy = pltpu.make_async_copy(w_hbm, w, wsem)
-    w_swap = remote(w_hbm, w, wss, wsr, dev(plane + y, turned))
-
-    @pl.when(same)
-    def _():
-        w_copy.start()
-
-    @pl.when(jnp.logical_not(same))
-    def _():
-        w_swap.start()
-
-    for i in range(2, nch):
-        span_chunk(i)
-
-    for h in range(HEADS):
-        rows = slice(h * SPAN, (h + 1) * SPAN)
-        span_ref[0, :, h * HD:(h + 1) * HD] = (acc_s[rows, 0:HD] / acc_s[rows, HD:]).astype(jnp.bfloat16)
 
     for o in NEAR[1:]:
         slot = yo(-o)
@@ -169,11 +181,11 @@
 
     owner_of = (iota((16, HD), 0) & 7) // 2
     sent2 = []
-    for o in (1, 7, 2, 6, 3, 5, 4, 0):
+    for o in (6, 2, 5, 7, 1, 3, 4, 0):
         to = lax.rem(block + o, NZL * NX)
         own = jnp.zeros((16, HD), jnp.float32)
         for j in range(4):
-            at = groups[to * NY + y, j] & (NY - 1)
+            at = groups[j, to * NY + y] & (NY - 1)
             s2[to, j * 16:(j + 1) * 16, :] = g1[at, j * 16:(j + 1) * 16, :]
             own = jnp.where(owner_of == j, g1[at, 64:80, :].astype(jnp.float32), own)
         s2[to, 64:80, :] = own.astype(jnp.bfloat16)
@@ -183,29 +195,14 @@
             sent2.append(c)
     r2[block] = s2[block]
 
-    lane = iota((16, 512), 1)
-    sub = iota((16, 512), 0)
-    col = (sub & 7) // 2
-
-    def one_hot(i, _):
-        want = jnp.zeros((16, 512), jnp.int32)
-        for half in range(2):
-            for j in range(4):
-                want = jnp.where(
-                    jnp.logical_and(sub // 8 == half, col == j), groups[2 * i + half, j], want
-                )
-        hit = want * 8 + (sub & 7) == lane
-        pt[pl.ds(pl.multiple_of(i * 16, 16), 16), :] = jnp.where(hit, 1.0, 0.0).astype(jnp.bfloat16)
-        return 0
-
-    lax.fori_loop(0, 32, one_hot, 0)
+    span_chunk(nch - 1)
 
     for o in range(1, NZL * NX):
         slot = lax.rem(block + NZL * NX - o, NZL * NX)
         remote(s2.at[slot], r2.at[slot], g2s.at[o], g2r.at[o], dev(slot * NY + y, tp)).wait_recv()
     own = jnp.zeros((16, HD), jnp.float32)
     for j in range(4):
-        at = lax.shift_right_logical(groups[section, j], 3)
+        at = lax.shift_right_logical(groups[j, section], 3)
         qf[j * 16:(j + 1) * 16, :] = r2[at, j * 16:(j + 1) * 16, :].astype(jnp.float32)
         own = jnp.where(owner_of == j, r2[at, 64:80, :].astype(jnp.float32), own)
 
@@ -217,7 +214,7 @@
     own_v = jnp.concatenate([own[8:16], own[0:8]], axis=0).astype(jnp.bfloat16)
     own_v = jnp.concatenate([own_v, jnp.ones((16, HD), jnp.bfloat16)], axis=1)
     s_ctx = dot(query, k[...], NT)
-    s_blk = dot(query, sk[0], NT)
+    s_blk = dot(query, sk[...], NT)
     s_own = dot(query, own_k, NT)
     r16, c16 = iota((64, 16), 0), iota((64, 16), 1)
     fits = jnp.logical_and(c16 // 2 == (r16 // 2) % 4, c16 % 2 <= r16 % 2)
@@ -244,8 +241,30 @@
             def _():
                 buf[section] = msg[...]
 
-    def sibling(slot, i):
-        return remote(buf.at[slot], buf.at[slot], cs.at[i], cr.at[i], dev(section, zh * 2 + 1 - core))
+    for h in range(HEADS):
+        rows = slice(h * SPAN, (h + 1) * SPAN)
+        span_ref[0, :, h * HD:(h + 1) * HD] = (acc_s[rows, 0:HD] / acc_s[rows, HD:]).astype(jnp.bfloat16)
+
+    lane = iota((16, 512), 1)
+    sub = iota((16, 512), 0)
+    col = (sub & 7) // 2
+
+    def one_hot(i, _):
+        want = jnp.zeros((16, 512), jnp.int32)
+        for half in range(2):
+            for j in range(4):
+                want = jnp.where(
+                    jnp.logical_and(sub // 8 == half, col == j), groups[j, 2 * i + half], want
+                )
+        hit = ((want * 8 + (sub & 7) + (NZH - zh) * 128) & 511) == lane
+        pt[pl.ds(pl.multiple_of(i * 16, 16), 16), :] = jnp.where(hit, 1.0, 0.0).astype(jnp.bfloat16)
+        return 0
+
+    lax.fori_loop(0, 32, one_hot, 0)
+
+    def sibling(half, o):
+        part = buf4.at[half, :, yo(-o)]
+        return remote(part, part, cs.at[o], cr.at[o], dev(section, zh * 2 + 1 - core))
 
     for o in NEAR:
         slot = plane + yo(-o)
@@ -254,16 +273,13 @@
             c.wait_recv()
         else:
             pl.when(jnp.logical_not(same))(c.wait_recv)
-        for d in NEAR_X:
+        for d in (2, 1, 3):
             c = remote(
                 buf.at[slot], buf.at[slot], p2s.at[o, d], p2r.at[o, d],
                 dev(zl * 32 + xo(d) * NY + y, tp),
             )
             c.start()
             sent3.append(c)
-        c = sibling(slot, o * 4)
-        c.start()
-        sent3.append(c)
     for o in NEAR:
         for d in NEAR_X:
             slot = core * 32 + xo(-d) * NY + yo(-o)
@@ -271,39 +287,50 @@
                 buf.at[slot], buf.at[slot], p2s.at[o, d], p2r.at[o, d],
                 dev(zl * 32 + xo(d) * NY + y, tp),
             ).wait_recv()
-            c = sibling(slot, o * 4 + d)
-            c.start()
-            sent3.append(c)
-    for o in NEAR:
-        for d in (0, *NEAR_X):
-            slot = (1 - core) * 32 + xo(-d) * NY + yo(-o)
-            sibling(slot, o * 4 + d).wait_recv()
-
+        c = sibling(core, o)
+        c.start()
+        sent3.append(c)
     pl.when(same)(w_copy.wait)
     pl.when(jnp.logical_not(same))(w_swap.wait_recv)
-    full = None
-    for pair in range(HEADS // 2):
-        at = pair * 2 * HD
-        both = jnp.concatenate([w[at:at + HD, :], w[at + HD:at + 2 * HD, :]], axis=1)
-        part = dot(buf[:, pair * 16:(pair + 1) * 16, :].reshape(1024, HD), both)
-        full = part if full is None else full + part
-    full = full.reshape(64, 16, 2 * HD)
-    rows = (full[:, 0:8, 0:HD] + full[:, 8:16, HD:]).reshape(512, HD).astype(jnp.bfloat16)
-    zs[...] = dot(pt[...], rows, TN).astype(jnp.bfloat16)
+
+    def project(half):
+        full = None
+        for pair in range(HEADS // 2):
+            at = pair * 2 * HD
+            both = jnp.concatenate([w[at:at + HD, :], w[at + HD:at + 2 * HD, :]], axis=1)
+            x_pair = buf[pl.ds(half * 32, 32), pair * 16:(pair + 1) * 16, :].reshape(512, HD)
+            part = dot(x_pair, both)
+            full = part if full is None else full + part
+        full = full.reshape(32, 16, 2 * HD)
+        rows = (full[:, 0:8, 0:HD] + full[:, 8:16, HD:]).reshape(256, HD)
+        zp[pl.ds(pl.multiple_of(half * 256, 256), 256), :] = rows.astype(jnp.bfloat16)
+
+    project(core)
+    for o in NEAR:
+        sibling(1 - core, o).wait_recv()
+    project(1 - core)
 
     sent4 = []
-    for t in range(8):
-        c = remote(
-            zs.at[pl.ds(t * 64, 64)], rr.at[turned], rs.at[t], rrs.at[turned], dev(plane + y, t)
-        )
-        mine = jnp.logical_and(same, tp == t)
-        pl.when(jnp.logical_not(mine))(c.start)
-
-        @pl.when(mine)
-        def _(t=t):
-            rr[turned] = zs[t * 64:(t + 1) * 64, :]
-
-        sent4.append((c, mine))
+    for hh in (2, 1, 3, 0):
+        rows = dot(pt[:, hh * 128:(hh + 1) * 128], zp[...], TN)
+        zs[hh * 128:(hh + 1) * 128, :] = rows.astype(jnp.bfloat16)
+        for e in range(2):
+            at = pl.ds(hh * 128 + e * 64, 64)
+            to = lax.rem(zh + hh, NZH) * 2 + e
+            c = remote(zs.at[at], rr.at[turned], rs.at[hh * 2 + e], rrs.at[turned], dev(plane + y, to))
+            if hh:
+                c.start()
+                sent4.append(c.wait_send)
+                continue
+            mine = jnp.logical_and(same, core == e)
+            other = jnp.logical_not(mine)
+            pl.when(other)(c.start)
+            sent4.append(functools.partial(pl.when(other), c.wait_send))
+
+            @pl.when(mine)
+            def _():
+                rr[turned] = zs[at, :]
+
     out = None
     for s in range(8):
         c = remote(zs.at[pl.ds(s * 64, 64)], rr.at[s], rs.at[s], rrs.at[s], dev(plane + y, s))
@@ -318,30 +345,36 @@
     pl.when(jnp.logical_not(same))(w_swap.wait_send)
     c = remote(msg, buf.at[section], p1s.at[0], p1r.at[0], dev(plane + y, turned))
     pl.when(jnp.logical_not(same))(c.wait_send)
-    for c, mine in sent4:
-        pl.when(jnp.logical_not(mine))(c.wait_send)
+    for wait in sent4:
+        wait()
 
 
 def body(ctx_keys, ctx_values, span_q, span_k, span_v, lengths, group_lists, dec_q, dec_k, dec_v, out_weight):
     ctx = ctx_keys.shape[1]
     bf, f32 = jnp.bfloat16, jnp.float32
     vmem = pl.BlockSpec(memory_space=pltpu.VMEM)
-    smem = pl.BlockSpec(memory_space=pltpu.SMEM)
-    hbm = pl.BlockSpec(memory_space=pltpu.HBM)
+    hbm = pl.BlockSpec(memory_space=pl.ANY)
     dma = pltpu.SemaphoreType.DMA
     span_out, proj = pl.pallas_call(
         kernel,
         name="block_and_decode_attention",
         out_shape=(
-            jax.ShapeDtypeStruct(span_q.shape, bf),
-            jax.ShapeDtypeStruct((64, HD), bf),
+            pltpu.VMEM(span_q.shape, bf),
+            pltpu.VMEM((64, HD), bf),
         ),
-        in_specs=[hbm, hbm, vmem, vmem, vmem, smem, smem, vmem, vmem, vmem, hbm],
+        in_specs=[pl.BlockSpec(memory_space=pltpu.SMEM)] + [hbm] * 10,
         out_specs=(vmem, vmem),
         scratch_shapes=[
+            pltpu.VMEM((SPAN, HEADS * HD), bf),
+            pltpu.VMEM((SPAN, HD), bf),
+            pltpu.VMEM((SPAN, 2 * HD), bf),
+            pltpu.SMEM((4, 64), jnp.int32),
+            pltpu.VMEM(dec_q.shape, bf),
+            pltpu.VMEM(dec_k.shape, bf),
+            pltpu.VMEM(dec_v.shape, bf),
+            dma((8,)),
             pltpu.VMEM((ctx, HD), bf),
             pltpu.VMEM((ctx, 2 * HD), bf),
-            pltpu.VMEM((SPAN, 2 * HD), bf),
             pltpu.VMEM((HEADS * SPAN, HD), bf),
             pltpu.VMEM((HEADS * SPAN, HD), f32),
             pltpu.VMEM((HEADS * SPAN, 2 * HD), f32),
@@ -356,18 +389,25 @@
             pltpu.VMEM((HEADS * HD, HD), bf),
             pltpu.VMEM((512, 512), bf),
             pltpu.VMEM((512, HD), bf),
+            pltpu.VMEM((512, HD), bf),
             pltpu.VMEM((8, 64, HD), bf),
             dma((ctx // CHUNK,)), dma((ctx // CHUNK,)), dma,
             dma((8,)), dma((8,)), dma((8,)), dma((8,)), dma, dma,
-            dma((8,)), dma((8,)), dma((8, 4)), dma((8, 4)), dma((32,)), dma((32,)),
+            dma((8,)), dma((8,)), dma((8, 4)), dma((8, 4)), dma((8,)), dma((8,)),
             dma((8,)), dma((8,)),
         ],
         compiler_params=pltpu.CompilerParams(
-            collective_id=0, has_side_effects=True, vmem_limit_bytes=48 << 20
+            collective_id=0, has_side_effects=True, vmem_limit_bytes=58 << 20
         ),
         cost_estimate=pl.CostEstimate(flops=2_000_000_000, bytes_accessed=4 << 20, transcendentals=3_600_000),
     )(
-        ctx_keys, ctx_values, span_q, span_k, span_v, lengths, group_lists, dec_q, dec_k, dec_v, out_weight
+        lengths,
+        *(
+            pltpu.with_memory_space_constraint(a, pltpu.HBM)
+            for a in (
+                ctx_keys, ctx_values, span_q, span_k, span_v, group_lists.T, dec_q, dec_k, dec_v, out_weight
+            )
+        ),
     )
     return span_out, proj.reshape(32, 2, HD)
 

time: 63.3 us -> 52.7 us (0.83)
  local copies, waits for them, and re-layouts: 10.2 us -> 1.26 us
  Pallas kernels: 51.3 us -> 50 us
    unnamed x21 -> x2, local copies, waits for them, and re-layouts: 10.2 us -> 1.26 us
    pallas_call x1, Pallas kernels: 51.3 us -> 50 us  [body(): pl.pallas_call(kernel, name='block_and_decode_attention', out_shape=(pltp...]
where the time goes in v2:
time: 52.7 us; the launch traced here: 52.6 us
  Pallas kernels  50 us (95%)
  between operations  1.29 us (2%)
  local copies, waits for them, and re-layouts  1.26 us (2%)
    pallas_call x1, Pallas kernels, body(): pl.pallas_call(kernel, name='block_and_decode_attention', out_shape=(pltp...  50 us
    unnamed x2, local copies, waits for them, and re-layouts  1.26 us

profile of v2, /device:TPU:1, one launch (start us, length us, event | category | flops | bytes accessed | tf_op | source)
XLA Modules:
  0.0 52.6 jit_solution(3531639569087295999)
XLA Ops:
  1.3 50.0 %block_and_decode_attention.1 = (bf16[1,64,1024]{2,1,0:T(8,128)(2,1)S(1)}, bf16[64,128]{1,0:T(8,128)(2,1)S(1)}) custom-call(s32[1]{0:T(128)S(6)} %copy.17.length_ref, bf16[1,6144,128]{2,1,0:T(8,128)(2,1)} %ck.1, bf16[1,6144,128]{2,1,0:T(8,128)(2,1)} %cv.1, bf16[1,64,1024]{2,1,0:T(8,128)(2,1)} %sq_hbm.1, bf16[1,64,128]{2,1,0:T(8,128)(2,1)} %sk_hbm.1, ...), custom_call_target="tpu_custom_call" | custom-call | flops 2000000000 | bytes 4194304 | tf_op jit(solution)/shard_map/block_and_decode_attention/pallas_call | solution.py:358
  51.3 0.7 %copy.15 = bf16[1,64,1024]{2,1,0:T(8,128)(2,1)} copy(bf16[1,64,1024]{2,1,0:T(8,128)(2,1)S(1)} %get-tuple-element.6) | data formatting | bytes 262144
  52.0 0.6 %copy.16 = bf16[32,2,128]{2,1,0:T(2,128)(2,1)} copy(bf16[32,2,128]{2,1,0:T(2,128)(2,1)S(1)} %bitcast.2) | data formatting | bytes 32768

commit v3 on v2

--- a/solution.py
+++ b/solution.py
@@ -153,16 +153,18 @@
     m_s[...] = jnp.broadcast_to(top, m_s.shape)
     length = length_ref[0]
 
-    def span_chunk(i):
+    def prepare(i):
         rows = pl.ds(i * CHUNK, CHUNK)
         for c in chunk_copies(i):
             c.wait()
         seen = jnp.where(iota((CHUNK, HD), 0) + i * CHUNK < length, 1.0, 0.0).astype(jnp.bfloat16)
-        kc = k[rows, :] * seen + k[0:1, :] * (1 - seen)
-        k[rows, :] = kc
+        k[rows, :] = k[rows, :] * seen + k[0:1, :] * (1 - seen)
         v[rows, 0:HD] = v[rows, 0:HD] * seen
         v[rows, HD:] = seen
-        s = dot(qs[...], kc, NT)
+
+    def span_chunk(i):
+        rows = pl.ds(i * CHUNK, CHUNK)
+        s = dot(qs[...], k[rows, :], NT)
         old = m_s[...]
         new = jnp.maximum(old, jnp.max(s, axis=1, keepdims=True) * LOG2)
         p = jnp.exp2(s * LOG2 - new[:, 0:1])
@@ -172,7 +174,8 @@
         acc_s[:, 0:HD] = acc_s[:, 0:HD] * shrink + part[:, 0:HD]
         acc_s[:, HD:] = acc_s[:, HD:] * shrink + part[:, HD:]
 
-    for i in range(nch - 1):
+    for i in range(3):
+        prepare(i)
         span_chunk(i)
 
     for o in NEAR[1:]:
@@ -195,7 +198,10 @@
             sent2.append(c)
     r2[block] = s2[block]
 
-    span_chunk(nch - 1)
+    for i in range(3, nch):
+        prepare(i)
+    for i in range(3, 5):
+        span_chunk(i)
 
     for o in range(1, NZL * NX):
         slot = lax.rem(block + NZL * NX - o, NZL * NX)
@@ -241,6 +247,8 @@
             def _():
                 buf[section] = msg[...]
 
+    for i in range(5, nch):
+        span_chunk(i)
     for h in range(HEADS):
         rows = slice(h * SPAN, (h + 1) * SPAN)
         span_ref[0, :, h * HD:(h + 1) * HD] = (acc_s[rows, 0:HD] / acc_s[rows, HD:]).astype(jnp.bfloat16)

time: 52.7 us -> 51 us (0.968)
  Pallas kernels: 50 us -> 48.3 us
    pallas_call x1, Pallas kernels: 50 us -> 48.3 us  [body(): pl.pallas_call(kernel, name='block_and_decode_attention', out_shape=(pltp...]
where the time goes in v3:
time: 51 us; the launch traced here: 50.8 us
  Pallas kernels  48.3 us (95%)
  between operations  1.29 us (3%)
  local copies, waits for them, and re-layouts  1.26 us (2%)
    pallas_call x1, Pallas kernels, body(): pl.pallas_call(kernel, name='block_and_decode_attention', out_shape=(pltp...  48.3 us
    unnamed x2, local copies, waits for them, and re-layouts  1.26 us

profile of v3, /device:TPU:1, one launch (start us, length us, event | category | flops | bytes accessed | tf_op | source)
XLA Modules:
  0.0 50.8 jit_solution(13037963366605092299)
XLA Ops:
  1.3 48.3 %block_and_decode_attention.1 = (bf16[1,64,1024]{2,1,0:T(8,128)(2,1)S(1)}, bf16[64,128]{1,0:T(8,128)(2,1)S(1)}) custom-call(s32[1]{0:T(128)S(6)} %copy.17.length_ref, bf16[1,6144,128]{2,1,0:T(8,128)(2,1)} %ck.1, bf16[1,6144,128]{2,1,0:T(8,128)(2,1)} %cv.1, bf16[1,64,1024]{2,1,0:T(8,128)(2,1)} %sq_hbm.1, bf16[1,64,128]{2,1,0:T(8,128)(2,1)} %sk_hbm.1, ...), custom_call_target="tpu_custom_call" | custom-call | flops 2000000000 | bytes 4194304 | tf_op jit(solution)/shard_map/block_and_decode_attention/pallas_call | solution.py:366
  49.5 0.7 %copy.15 = bf16[1,64,1024]{2,1,0:T(8,128)(2,1)} copy(bf16[1,64,1024]{2,1,0:T(8,128)(2,1)S(1)} %get-tuple-element.6) | data formatting | bytes 262144
  50.2 0.6 %copy.16 = bf16[32,2,128]{2,1,0:T(2,128)(2,1)} copy(bf16[32,2,128]{2,1,0:T(2,128)(2,1)S(1)} %bitcast.2) | data formatting | bytes 32768

commit v4 on v3

--- a/solution.py
+++ b/solution.py
@@ -174,7 +174,7 @@
         acc_s[:, 0:HD] = acc_s[:, 0:HD] * shrink + part[:, 0:HD]
         acc_s[:, HD:] = acc_s[:, HD:] * shrink + part[:, HD:]
 
-    for i in range(3):
+    for i in range(2):
         prepare(i)
         span_chunk(i)
 
@@ -198,9 +198,9 @@
             sent2.append(c)
     r2[block] = s2[block]
 
-    for i in range(3, nch):
+    for i in range(2, nch):
         prepare(i)
-    for i in range(3, 5):
+    for i in range(2, 5):
         span_chunk(i)
 
     for o in range(1, NZL * NX):
@@ -343,7 +343,6 @@
     for s in range(8):
         c = remote(zs.at[pl.ds(s * 64, 64)], rr.at[s], rs.at[s], rrs.at[s], dev(plane + y, s))
         pl.when(jnp.logical_not(jnp.logical_and(same, turned == s)))(c.wait_recv)
-    for s in range(8):
         part = rr[s].astype(jnp.float32)
         out = part if out is None else out + part
     proj_ref[...] = out.astype(jnp.bfloat16)

time: 51 us -> 50.9 us (level)
  no operation moved by 1% of the time
where the time goes in v4:
time: 50.9 us; the launch traced here: 50.8 us
  Pallas kernels  48.2 us (95%)
  between operations  1.29 us (3%)
  local copies, waits for them, and re-layouts  1.26 us (2%)
    pallas_call x1, Pallas kernels, body(): pl.pallas_call(kernel, name='block_and_decode_attention', out_shape=(pltp...  48.2 us
    unnamed x2, local copies, waits for them, and re-layouts  1.26 us

profile of v4, /device:TPU:1, one launch (start us, length us, event | category | flops | bytes accessed | tf_op | source)
XLA Modules:
  0.0 50.8 jit_solution(12593923565107436558)
XLA Ops:
  1.3 48.2 %block_and_decode_attention.1 = (bf16[1,64,1024]{2,1,0:T(8,128)(2,1)S(1)}, bf16[64,128]{1,0:T(8,128)(2,1)S(1)}) custom-call(s32[1]{0:T(128)S(6)} %copy.17.length_ref, bf16[1,6144,128]{2,1,0:T(8,128)(2,1)} %ck.1, bf16[1,6144,128]{2,1,0:T(8,128)(2,1)} %cv.1, bf16[1,64,1024]{2,1,0:T(8,128)(2,1)} %sq_hbm.1, bf16[1,64,128]{2,1,0:T(8,128)(2,1)} %sk_hbm.1, ...), custom_call_target="tpu_custom_call" | custom-call | flops 2000000000 | bytes 4194304 | tf_op jit(solution)/shard_map/block_and_decode_attention/pallas_call | solution.py:365
  49.5 0.7 %copy.15 = bf16[1,64,1024]{2,1,0:T(8,128)(2,1)} copy(bf16[1,64,1024]{2,1,0:T(8,128)(2,1)S(1)} %get-tuple-element.6) | data formatting | bytes 262144
  50.2 0.6 %copy.16 = bf16[32,2,128]{2,1,0:T(2,128)(2,1)} copy(bf16[32,2,128]{2,1,0:T(2,128)(2,1)S(1)} %bitcast.2) | data formatting | bytes 32768
